TPU v7x, 512 devices: a whole 4x4x16 slice. The times are simulated.
512 devices in a mesh: gx: 32 (over z, core), gy: 16 (over y, x).
Axes of the slice: x: 4, y: 4, z: 16, core: 2. Of those that a mesh axis runs over, the one named last changes fastest.
Arguments:
- source: float32 [256, 2048, 256], P('gx', 'gy'), may hold values from -8 to 8
- density: float32 [256, 2048, 256], P('gx', 'gy'), may hold values from 0.08 to 1.7
Outputs:
- pressure: float32 [256, 2048, 256], P('gx', 'gy')
- residual: float32 [256, 2048, 256], P('gx', 'gy')
All inputs are finite; a program needn't handle non-finite values.
Results may differ from a plain program's by a relative error of at most 0.00021.
Values sent between devices are 32-bit elements; how exact they have to be, the bound alone decides.
A program may use at most 64 MiB of HBM per device.

v0:
```python
import jax
import jax.numpy as jnp
from jax import lax
from jax.sharding import PartitionSpec as P

ITERS = 2


def extended(shard, sides, width):
    for axis, dim in sides:
        devices, length = (lax.axis_size(axis), shard.shape[dim])
        up = [(i, (i + 1) % devices) for i in range(devices - 1)]
        down = [(j, i) for i, j in up]
        last = lax.slice_in_dim(shard, length - width, length, axis=dim)
        initial = lax.slice_in_dim(shard, 0, width, axis=dim)
        before = lax.ppermute(last, axis, up)
        after = lax.ppermute(initial, axis, down)
        shard = jnp.concatenate([before, shard, after], axis=dim)
    return shard


def neighbours(padded):
    return [
        padded[2:, 1:-1, 1:-1],
        padded[:-2, 1:-1, 1:-1],
        padded[1:-1, 2:, 1:-1],
        padded[1:-1, :-2, 1:-1],
        padded[1:-1, 1:-1, 2:],
        padded[1:-1, 1:-1, :-2],
    ]


def pad_depth(field):
    return jnp.pad(field, ((0, 0), (0, 0), (1, 1)))


def weights_from(center, padded):
    nearby = neighbours(pad_depth(padded))
    weights = [2.0 / jnp.where(center > 0, center + other, 1.0) for other in nearby]
    diag_sum = weights[0]
    for weight_one in weights[1:]:
        diag_sum = diag_sum + weight_one
    return (weights, lax.rsqrt(diag_sum))


def couple(padded, weights):
    nearby = neighbours(pad_depth(padded))
    total = weights[0] * nearby[0]
    for weight_one, other in zip(weights[1:], nearby[1:]):
        total = total + weight_one * other
    return total


def scaled_apply(field, weights, scale_inv):
    scaled = scale_inv * field
    padded = extended(scaled, (("gx", 0), ("gy", 1)), 1)
    return field - scale_inv * couple(padded, weights)


def inner_pair(residual, shadow):
    gamma_part = jnp.sum(residual * residual)
    delta_part = jnp.sum(shadow * residual)
    return lax.psum((gamma_part, delta_part), ("gx", "gy"))


def shards(source, density):
    rim_density = extended(density, (("gx", 0), ("gy", 1)), 1)
    weights, scale_inv = weights_from(density, rim_density)
    residual = scale_inv * source
    shadow = scaled_apply(residual, weights, scale_inv)
    solution = jnp.zeros_like(source)
    direction = jnp.zeros_like(source)
    along = jnp.zeros_like(source)
    pushed = jnp.zeros_like(source)
    gamma_old = jnp.float32(1.0)
    alpha_old = jnp.float32(1.0)
    for iteration in range(ITERS):
        gamma_now, delta_now = inner_pair(residual, shadow)
        fresh = scaled_apply(shadow, weights, scale_inv)
        if iteration == 0:
            beta_now = jnp.float32(0.0)
            alpha_now = gamma_now / delta_now
        else:
            beta_now = gamma_now / gamma_old
            alpha_now = gamma_now / (delta_now - beta_now * gamma_now / alpha_old)
        pushed = fresh + beta_now * pushed
        along = shadow + beta_now * along
        direction = residual + beta_now * direction
        solution = solution + alpha_now * direction
        residual = residual - alpha_now * along
        shadow = shadow - alpha_now * pushed
        gamma_old = gamma_now
        alpha_old = alpha_now
    return (scale_inv * solution, residual)


def solution(mesh):
    in_specs = (P("gx", "gy", None), P("gx", "gy", None))
    out_specs = (P("gx", "gy", None), P("gx", "gy", None))
    return jax.shard_map(shards, mesh=mesh, in_specs=in_specs, out_specs=out_specs, check_vma=False)
```

profile of v0, /device:TPU:1, one launch (start us, length us, event | category | flops | bytes accessed | tf_op | source)
XLA Modules:
  0.0 292.1 jit_solution(12491736023000275440)
XLA Ops:
  1.6 4.9 %collective-permute-start.1 = (f32[1,128,256]{2,1,0:T(8,128)S(1)}, f32[1,128,256]{2,1,0:T(8,128)S(1)}, u32[]{:S(2)}, u32[]{:S(2)}) collective-permute-start(f32[1,128,256]{2,1,0:T(8,128)S(1)} %get-tuple-element.30), channel_id=1, source_target_pairs={{0,16},{16,32},{32,48},{48,64},{64,80},{80,96},{96,112},{112,128},... | collective-permute-start | bytes 393224 | tf_op jit(solution)/shard_map/ppermute | solution.py:16
  6.6 5.1 %collective-permute-start = (f32[1,128,256]{2,1,0:T(8,128)S(1)}, f32[1,128,256]{2,1,0:T(8,128)S(1)}, u32[]{:S(2)}, u32[]{:S(2)}) collective-permute-start(f32[1,128,256]{2,1,0:T(8,128)S(1)} %get-tuple-element.29), channel_id=1, source_target_pairs={{16,0},{32,16},{48,32},{64,48},{80,64},{96,80},{112,96},{128,112},... | collective-permute-start | bytes 393224 | tf_op jit(solution)/shard_map/ppermute | solution.py:17
  11.7 1.3 constant_dynamic-update-slice_fusion.1
  13.1 2.9 collective-permute-start.3
  16.0 1.3 collective-permute-start.2
  17.3 3.1 %collective-permute-done.2 = f32[10,1,256]{2,1,0:T(1,128)S(1)} collective-permute-done((f32[10,1,256]{2,1,0:T(1,128)S(1)}, f32[10,1,256]{2,1,0:T(1,128)S(1)}, u32[]{:S(2)}, u32[]{:S(2)}) %collective-permute-start.2) | collective-permute-done | bytes 10272 | tf_op jit(solution)/shard_map/ppermute | solution.py:17
  21.2 2.2 fusion.43
  23.5 3.3 %collective-permute-start.5 = (f32[1,128,256]{2,1,0:T(8,128)S(1)}, f32[1,128,256]{2,1,0:T(8,128)S(1)}, u32[]{:S(2)}, u32[]{:S(2)}) collective-permute-start(f32[1,128,256]{2,1,0:T(8,128)S(1)} %get-tuple-element.27), channel_id=1, source_target_pairs={{0,16},{16,32},{32,48},{48,64},{64,80},{80,96},{96,112},{112,128},... | collective-permute-start | bytes 393224 | tf_op jit(solution)/shard_map/ppermute | solution.py:16
  26.8 1.9 collective-permute-start.4
  28.8 4.3 %collective-permute-done.4 = f32[1,128,256]{2,1,0:T(8,128)S(1)} collective-permute-done((f32[1,128,256]{2,1,0:T(8,128)S(1)}, f32[1,128,256]{2,1,0:T(8,128)S(1)}, u32[]{:S(2)}, u32[]{:S(2)}) %collective-permute-start.4) | collective-permute-done | bytes 131104 | tf_op jit(solution)/shard_map/ppermute | solution.py:17
  33.1 3.1 %collective-permute-start.7 = (f32[10,1,256]{2,1,0:T(1,128)S(1)}, f32[10,1,256]{2,1,0:T(1,128)S(1)}, u32[]{:S(2)}, u32[]{:S(2)}) collective-permute-start(f32[10,1,256]{2,1,0:T(1,128)S(1)} %get-tuple-element.21), channel_id=1, source_target_pairs={{0,1},{1,2},{2,3},{3,4},{4,5},{5,6},{6,7},{7,8},{8,9},{9,10},{10,1... | collective-permute-start | bytes 30728 | tf_op jit(solution)/shard_map/ppermute | solution.py:16
  36.3 1.3 collective-permute-start.6
  37.6 3.1 %collective-permute-done.6 = f32[10,1,256]{2,1,0:T(1,128)S(1)} collective-permute-done((f32[10,1,256]{2,1,0:T(1,128)S(1)}, f32[10,1,256]{2,1,0:T(1,128)S(1)}, u32[]{:S(2)}, u32[]{:S(2)}) %collective-permute-start.6) | collective-permute-done | bytes 10272 | tf_op jit(solution)/shard_map/ppermute | solution.py:17
  41.4 3.4 %multiply_reduce_fusion.2 = (f32[]{:T(128)}, f32[]{:T(128)}, f32[8,128,256]{2,1,0:T(8,128)S(1)}) fusion(f32[8,128,256]{2,1,0:T(8,128)S(1)} %get-tuple-element.13, f32[8,128,256]{2,1,0:T(8,128)S(1)} %get-tuple-element.14, f32[10,130,258]{2,1,0:T(8,128)S(1)} %select_maximum_fusion.4, f32[8,128,256]{2,1,0:T(8,128)S(1)} %copy-done, ...), kind=kLoop, calls=%fused_computation.84 | loop fusion | flops 10485758 | bytes 12079112 | tf_op jit(solution)/shard_map/reduce_sum | solution.py:62
  45.1 3.2 %collective-permute-start.9 = (f32[1,128,256]{2,1,0:T(8,128)S(1)}, f32[1,128,256]{2,1,0:T(8,128)S(1)}, u32[]{:S(2)}, u32[]{:S(2)}) collective-permute-start(f32[1,128,256]{2,1,0:T(8,128)S(1)} %get-tuple-element.25), channel_id=1, source_target_pairs={{0,16},{16,32},{32,48},{48,64},{64,80},{80,96},{96,112},{112,128},... | collective-permute-start | bytes 393224 | tf_op jit(solution)/shard_map/ppermute | solution.py:16
  48.3 1.9 collective-permute-start.8
  50.2 4.3 %collective-permute-done.8 = f32[1,128,256]{2,1,0:T(8,128)S(1)} collective-permute-done((f32[1,128,256]{2,1,0:T(8,128)S(1)}, f32[1,128,256]{2,1,0:T(8,128)S(1)}, u32[]{:S(2)}, u32[]{:S(2)}) %collective-permute-start.8) | collective-permute-done | bytes 131104 | tf_op jit(solution)/shard_map/ppermute | solution.py:17
  55.2 4.4 %collective-permute-start.11 = (f32[10,1,256]{2,1,0:T(1,128)}, f32[10,1,256]{2,1,0:T(1,128)S(1)}, u32[]{:S(2)}, u32[]{:S(2)}) collective-permute-start(f32[10,1,256]{2,1,0:T(1,128)} %get-tuple-element.19), channel_id=1, source_target_pairs={{0,1},{1,2},{2,3},{3,4},{4,5},{5,6},{6,7},{7,8},{8,9},{9,10},{10,1... | collective-permute-start | bytes 30728 | tf_op jit(solution)/shard_map/ppermute | solution.py:16
  59.6 1.3 collective-permute-start.10
  60.9 114.2 %all-reduce.4 = (f32[]{:T(128)}, f32[]{:T(128)}) all-reduce(f32[]{:T(128)} %get-tuple-element.5, f32[]{:T(128)} %get-tuple-element.4), channel_id=1, replica_groups=mesh['gx'=32,'gy'=16] {'gx','gy'}, use_global_device_ids=true, to_apply=%region_1.2 | all-reduce | flops 2 | bytes 16 | tf_op jit(solution)/shard_map/psum | solution.py:63
  176.5 2.2 select_maximum_fusion
  178.7 5.7 %multiply_reduce_fusion = (f32[]{:T(128)}, f32[]{:T(128)}, f32[8,128,256]{2,1,0:T(8,128)}) fusion(f32[8,128,256]{2,1,0:T(8,128)S(1)} %copy-done.5, f32[8,128,256]{2,1,0:T(8,128)} %copy-done.6, f32[]{:T(128)S(6)} %div.36, f32[8,128,256]{2,1,0:T(8,128)S(1)} %get-tuple-element.14, f32[10,130,258]{2,1,0:T(8,128)S(1)} %select_maximum_fusion, ...), kind=kLoop, calls=%fused_computation.81 | loop fusion | flops 11534334 | bytes 13127692 | tf_op jit(solution)/shard_map/reduce_sum | solution.py:62
  184.4 99.5 %all-reduce.3 = (f32[]{:T(128)}, f32[]{:T(128)}) all-reduce(f32[]{:T(128)} %get-tuple-element.3, f32[]{:T(128)} %get-tuple-element.2), channel_id=1, replica_groups=mesh['gx'=32,'gy'=16] {'gx','gy'}, use_global_device_ids=true, to_apply=%region_5.6 | all-reduce | flops 2 | bytes 16 | tf_op jit(solution)/shard_map/psum | solution.py:63
  288.5 3.6 %multiply_subtract_fusion = (f32[8,128,256]{2,1,0:T(8,128)}, f32[8,128,256]{2,1,0:T(8,128)}) fusion(f32[8,128,256]{2,1,0:T(8,128)} %get-tuple-element.10, f32[8,128,256]{2,1,0:T(8,128)} %copy-done.6, f32[]{:T(128)S(6)} %div.37, f32[]{:T(128)S(6)} %div.39, f32[8,128,256]{2,1,0:T(8,128)} %copy-done.4, f32[]{:T(128)S(6)} %div.36, ...), kind=kLoop, calls=%fused_computation.79 | loop fusion | flops 3145728 | bytes 6291468 | tf_op jit(solution)/shard_map/sub | solution.py:90
  (43 shorter events, 3.4 us)
Async XLA Ops:
  1.6 10.1 %collective-permute-start.1 = (f32[1,128,256]{2,1,0:T(8,128)S(1)}, f32[1,128,256]{2,1,0:T(8,128)S(1)}, u32[]{:S(2)}, u32[]{:S(2)}) collective-permute-start(f32[1,128,256]{2,1,0:T(8,128)S(1)} %get-tuple-element.30), channel_id=1, source_target_pairs={{0,16},{16,32},{32,48},{48,64},{64,80},{80,96},{96,112},{112,128},... | collective-permute-start | bytes 393224 | tf_op jit(solution)/shard_map/ppermute | solution.py:16
  6.6 6.5 %collective-permute-start = (f32[1,128,256]{2,1,0:T(8,128)S(1)}, f32[1,128,256]{2,1,0:T(8,128)S(1)}, u32[]{:S(2)}, u32[]{:S(2)}) collective-permute-start(f32[1,128,256]{2,1,0:T(8,128)S(1)} %get-tuple-element.29), channel_id=1, source_target_pairs={{16,0},{32,16},{48,32},{64,48},{80,64},{96,80},{112,96},{128,112},... | collective-permute-start | bytes 393224 | tf_op jit(solution)/shard_map/ppermute | solution.py:17
  13.1 8.1 %copy-start = (f32[8,128,256]{2,1,0:T(8,128)S(1)}, f32[8,128,256]{2,1,0:T(8,128)}, u32[]{:S(2)}) copy-start(f32[8,128,256]{2,1,0:T(8,128)} %param.3) | copy-start | bytes 3145732
  13.1 8.1 %copy-start.11 = (f32[8,128,256]{2,1,0:T(8,128)S(1)}, f32[8,128,256]{2,1,0:T(8,128)}, u32[]{:S(2)}) copy-start(f32[8,128,256]{2,1,0:T(8,128)} %param.2) | copy-start | bytes 3145732
  13.1 4.2 %collective-permute-start.3 = (f32[10,1,256]{2,1,0:T(1,128)S(1)}, f32[10,1,256]{2,1,0:T(1,128)S(1)}, u32[]{:S(2)}, u32[]{:S(2)}) collective-permute-start(f32[10,1,256]{2,1,0:T(1,128)S(1)} %get-tuple-element.23), channel_id=1, source_target_pairs={{0,1},{1,2},{2,3},{3,4},{4,5},{5,6},{6,7},{7,8},{8,9},{9,10},{10,1... | collective-permute-start | bytes 30728 | tf_op jit(solution)/shard_map/ppermute | solution.py:16
  16.0 4.4 %collective-permute-start.2 = (f32[10,1,256]{2,1,0:T(1,128)S(1)}, f32[10,1,256]{2,1,0:T(1,128)S(1)}, u32[]{:S(2)}, u32[]{:S(2)}) collective-permute-start(f32[10,1,256]{2,1,0:T(1,128)S(1)} %get-tuple-element.24), channel_id=1, source_target_pairs={{1,0},{2,1},{3,2},{4,3},{5,4},{6,5},{7,6},{8,7},{9,8},{10,9},{11,1... | collective-permute-start | bytes 30728 | tf_op jit(solution)/shard_map/ppermute | solution.py:17
  23.4 18.0 %copy-start.4 = (f32[8,128,256]{2,1,0:T(8,128)}, f32[8,128,256]{2,1,0:T(8,128)S(1)}, u32[]{:S(2)}) copy-start(f32[8,128,256]{2,1,0:T(8,128)S(1)} %get-tuple-element.13) | copy-start | bytes 3145732
  23.4 18.0 %copy-start.7 = (f32[8,128,256]{2,1,0:T(8,128)}, f32[8,128,256]{2,1,0:T(8,128)S(1)}, u32[]{:S(2)}) copy-start(f32[8,128,256]{2,1,0:T(8,128)S(1)} %get-tuple-element.15) | copy-start | bytes 3145732
  23.4 18.0 %copy-start.8 = (f32[8,128,256]{2,1,0:T(8,128)}, f32[8,128,256]{2,1,0:T(8,128)S(1)}, u32[]{:S(2)}) copy-start(f32[8,128,256]{2,1,0:T(8,128)S(1)} %get-tuple-element.16) | copy-start | bytes 3145732
  23.5 5.3 %collective-permute-start.5 = (f32[1,128,256]{2,1,0:T(8,128)S(1)}, f32[1,128,256]{2,1,0:T(8,128)S(1)}, u32[]{:S(2)}, u32[]{:S(2)}) collective-permute-start(f32[1,128,256]{2,1,0:T(8,128)S(1)} %get-tuple-element.27), channel_id=1, source_target_pairs={{0,16},{16,32},{32,48},{48,64},{64,80},{80,96},{96,112},{112,128},... | collective-permute-start | bytes 393224 | tf_op jit(solution)/shard_map/ppermute | solution.py:16
  26.8 6.3 %collective-permute-start.4 = (f32[1,128,256]{2,1,0:T(8,128)S(1)}, f32[1,128,256]{2,1,0:T(8,128)S(1)}, u32[]{:S(2)}, u32[]{:S(2)}) collective-permute-start(f32[1,128,256]{2,1,0:T(8,128)S(1)} %get-tuple-element.28), channel_id=1, source_target_pairs={{16,0},{32,16},{48,32},{64,48},{80,64},{96,80},{112,96},{128,112},... | collective-permute-start | bytes 393224 | tf_op jit(solution)/shard_map/ppermute | solution.py:17
  33.1 4.4 %collective-permute-start.7 = (f32[10,1,256]{2,1,0:T(1,128)S(1)}, f32[10,1,256]{2,1,0:T(1,128)S(1)}, u32[]{:S(2)}, u32[]{:S(2)}) collective-permute-start(f32[10,1,256]{2,1,0:T(1,128)S(1)} %get-tuple-element.21), channel_id=1, source_target_pairs={{0,1},{1,2},{2,3},{3,4},{4,5},{5,6},{6,7},{7,8},{8,9},{9,10},{10,1... | collective-permute-start | bytes 30728 | tf_op jit(solution)/shard_map/ppermute | solution.py:16
  36.3 4.4 %collective-permute-start.6 = (f32[10,1,256]{2,1,0:T(1,128)S(1)}, f32[10,1,256]{2,1,0:T(1,128)S(1)}, u32[]{:S(2)}, u32[]{:S(2)}) collective-permute-start(f32[10,1,256]{2,1,0:T(1,128)S(1)} %get-tuple-element.22), channel_id=1, source_target_pairs={{1,0},{2,1},{3,2},{4,3},{5,4},{6,5},{7,6},{8,7},{9,8},{10,9},{11,1... | collective-permute-start | bytes 30728 | tf_op jit(solution)/shard_map/ppermute | solution.py:17
  44.9 10.4 %copy-start.6 = (f32[8,128,256]{2,1,0:T(8,128)}, f32[8,128,256]{2,1,0:T(8,128)S(1)}, u32[]{:S(2)}) copy-start(f32[8,128,256]{2,1,0:T(8,128)S(1)} %get-tuple-element.11) | copy-start | bytes 3145732
  45.0 9.5 %copy-start.2 = (f32[8,128,256]{2,1,0:T(8,128)}, f32[8,128,256]{2,1,0:T(8,128)S(1)}, u32[]{:S(2)}) copy-start(f32[8,128,256]{2,1,0:T(8,128)S(1)} %mul.118) | copy-start | bytes 3145732
  45.1 5.2 %collective-permute-start.9 = (f32[1,128,256]{2,1,0:T(8,128)S(1)}, f32[1,128,256]{2,1,0:T(8,128)S(1)}, u32[]{:S(2)}, u32[]{:S(2)}) collective-permute-start(f32[1,128,256]{2,1,0:T(8,128)S(1)} %get-tuple-element.25), channel_id=1, source_target_pairs={{0,16},{16,32},{32,48},{48,64},{64,80},{80,96},{96,112},{112,128},... | collective-permute-start | bytes 393224 | tf_op jit(solution)/shard_map/ppermute | solution.py:16
  48.3 6.3 %collective-permute-start.8 = (f32[1,128,256]{2,1,0:T(8,128)S(1)}, f32[1,128,256]{2,1,0:T(8,128)S(1)}, u32[]{:S(2)}, u32[]{:S(2)}) collective-permute-start(f32[1,128,256]{2,1,0:T(8,128)S(1)} %get-tuple-element.26), channel_id=1, source_target_pairs={{16,0},{32,16},{48,32},{64,48},{80,64},{96,80},{112,96},{128,112},... | collective-permute-start | bytes 393224 | tf_op jit(solution)/shard_map/ppermute | solution.py:17
  54.6 0.7 copy-start.9
  55.2 121.2 %collective-permute-start.11 = (f32[10,1,256]{2,1,0:T(1,128)}, f32[10,1,256]{2,1,0:T(1,128)S(1)}, u32[]{:S(2)}, u32[]{:S(2)}) collective-permute-start(f32[10,1,256]{2,1,0:T(1,128)} %get-tuple-element.19), channel_id=1, source_target_pairs={{0,1},{1,2},{2,3},{3,4},{4,5},{5,6},{6,7},{7,8},{8,9},{9,10},{10,1... | collective-permute-start | bytes 30728 | tf_op jit(solution)/shard_map/ppermute | solution.py:16
  59.6 116.8 %collective-permute-start.10 = (f32[10,1,256]{2,1,0:T(1,128)}, f32[10,1,256]{2,1,0:T(1,128)S(1)}, u32[]{:S(2)}, u32[]{:S(2)}) collective-permute-start(f32[10,1,256]{2,1,0:T(1,128)} %get-tuple-element.20), channel_id=1, source_target_pairs={{1,0},{2,1},{3,2},{4,3},{5,4},{6,5},{7,6},{8,7},{9,8},{10,9},{11,1... | collective-permute-start | bytes 30728 | tf_op jit(solution)/shard_map/ppermute | solution.py:17
  176.4 2.2 copy-start.1
  176.4 2.2 copy-start.3
  176.4 2.2 copy-start.5
  176.4 2.2 copy-start.10
where the time goes:
time: 293 us; the launch traced here: 292 us
  blocking collectives  214 us (73%)
  starting transfers between devices  34.8 us (12%)
  other arithmetic  19.4 us (7%)
  waiting for transfers between devices  14.9 us (5%)
  between operations  6.86 us (2%)
    psum x2, blocking collectives, inner_pair(): return lax.psum((gamma_part, delta_part), ('gx', 'gy'))  214 us
    ppermute x6, starting transfers between devices, extended(): before = lax.ppermute(last, axis, up)  21.9 us
    ppermute x6, waiting for transfers between devices, extended(): after = lax.ppermute(initial, axis, down)  14.9 us
    ppermute x6, starting transfers between devices, extended(): after = lax.ppermute(initial, axis, down)  12.9 us
    reduce_sum x2, other arithmetic, inner_pair(): delta_part = jnp.sum(shadow * residual)  9.11 us
  transfers between devices with their start and end apart: 12, of which 4 were waited for; matrix products, arithmetic and copies ran while one was open for 0% of the time, Pallas kernels for 0%

commit v1 on v0

--- a/solution.py
+++ b/solution.py
@@ -60,7 +60,15 @@
 def inner_pair(residual, shadow):
     gamma_part = jnp.sum(residual * residual)
     delta_part = jnp.sum(shadow * residual)
-    return lax.psum((gamma_part, delta_part), ("gx", "gy"))
+
+    def matrix_group(x_in):
+        shard_axis = "gx"
+        link_axis = "gy"
+        for num in (link_axis, shard_axis):
+            x_in = lax.psum(x_in, num)
+        return x_in
+
+    return matrix_group((gamma_part, delta_part))
 
 
 def shards(source, density):

time: 293 us -> 250 us (0.85)
  blocking collectives: 214 us -> 172 us
    psum x2 -> x4, blocking collectives: 214 us -> 172 us  [matrix_group(): x_in = lax.psum(x_in, num)]
  transfers between devices with their start and end apart: 12 -> 12, of which waited for: 4 -> 4; matrix products, arithmetic and copies ran while one was open for 0% -> 1% of each run, Pallas kernels for 0% -> 0%
where the time goes in v1:
time: 250 us; the launch traced here: 249 us
  blocking collectives  172 us (69%)
  starting transfers between devices  34.8 us (14%)
  other arithmetic  19.3 us (8%)
  waiting for transfers between devices  14.9 us (6%)
  between operations  6.36 us (3%)
    psum x4, blocking collectives, matrix_group(): x_in = lax.psum(x_in, num)  172 us
    ppermute x6, starting transfers between devices, extended(): before = lax.ppermute(last, axis, up)  21.9 us
    ppermute x6, waiting for transfers between devices, extended(): after = lax.ppermute(initial, axis, down)  14.9 us
    ppermute x6, starting transfers between devices, extended(): after = lax.ppermute(initial, axis, down)  12.9 us
    reduce_sum x2, other arithmetic, inner_pair(): delta_part = jnp.sum(shadow * residual)  9 us
  transfers between devices with their start and end apart: 12, of which 4 were waited for; matrix products, arithmetic and copies ran while one was open for 1% of the time, Pallas kernels for 0%

profile of v1, /device:TPU:1, one launch (start us, length us, event | category | flops | bytes accessed | tf_op | source)
XLA Modules:
  0.0 249.3 jit_solution(16119182951761778702)
XLA Ops:
  1.6 4.9 %collective-permute-start.1 = (f32[1,128,256]{2,1,0:T(8,128)S(1)}, f32[1,128,256]{2,1,0:T(8,128)S(1)}, u32[]{:S(2)}, u32[]{:S(2)}) collective-permute-start(f32[1,128,256]{2,1,0:T(8,128)S(1)} %get-tuple-element.34), channel_id=1, source_target_pairs={{0,16},{16,32},{32,48},{48,64},{64,80},{80,96},{96,112},{112,128},... | collective-permute-start | bytes 393224 | tf_op jit(solution)/shard_map/ppermute | solution.py:16
  6.6 5.1 %collective-permute-start = (f32[1,128,256]{2,1,0:T(8,128)S(1)}, f32[1,128,256]{2,1,0:T(8,128)S(1)}, u32[]{:S(2)}, u32[]{:S(2)}) collective-permute-start(f32[1,128,256]{2,1,0:T(8,128)S(1)} %get-tuple-element.33), channel_id=1, source_target_pairs={{16,0},{32,16},{48,32},{64,48},{80,64},{96,80},{112,96},{128,112},... | collective-permute-start | bytes 393224 | tf_op jit(solution)/shard_map/ppermute | solution.py:17
  11.7 1.3 constant_dynamic-update-slice_fusion.1
  13.1 2.9 %collective-permute-start.3 = (f32[10,1,256]{2,1,0:T(1,128)S(1)}, f32[10,1,256]{2,1,0:T(1,128)S(1)}, u32[]{:S(2)}, u32[]{:S(2)}) collective-permute-start(f32[10,1,256]{2,1,0:T(1,128)S(1)} %get-tuple-element.27), channel_id=1, source_target_pairs={{0,1},{1,2},{2,3},{3,4},{4,5},{5,6},{6,7},{7,8},{8,9},{9,10},{10,1... | collective-permute-start | bytes 30728 | tf_op jit(solution)/shard_map/ppermute | solution.py:16
  16.0 1.3 collective-permute-start.2
  17.3 3.1 %collective-permute-done.2 = f32[10,1,256]{2,1,0:T(1,128)S(1)} collective-permute-done((f32[10,1,256]{2,1,0:T(1,128)S(1)}, f32[10,1,256]{2,1,0:T(1,128)S(1)}, u32[]{:S(2)}, u32[]{:S(2)}) %collective-permute-start.2) | collective-permute-done | bytes 10272 | tf_op jit(solution)/shard_map/ppermute | solution.py:17
  21.2 2.2 fusion.43
  23.5 3.3 %collective-permute-start.5 = (f32[1,128,256]{2,1,0:T(8,128)S(1)}, f32[1,128,256]{2,1,0:T(8,128)S(1)}, u32[]{:S(2)}, u32[]{:S(2)}) collective-permute-start(f32[1,128,256]{2,1,0:T(8,128)S(1)} %get-tuple-element.31), channel_id=1, source_target_pairs={{0,16},{16,32},{32,48},{48,64},{64,80},{80,96},{96,112},{112,128},... | collective-permute-start | bytes 393224 | tf_op jit(solution)/shard_map/ppermute | solution.py:16
  26.8 1.9 collective-permute-start.4
  28.8 4.3 %collective-permute-done.4 = f32[1,128,256]{2,1,0:T(8,128)S(1)} collective-permute-done((f32[1,128,256]{2,1,0:T(8,128)S(1)}, f32[1,128,256]{2,1,0:T(8,128)S(1)}, u32[]{:S(2)}, u32[]{:S(2)}) %collective-permute-start.4) | collective-permute-done | bytes 131104 | tf_op jit(solution)/shard_map/ppermute | solution.py:17
  33.1 3.1 %collective-permute-start.7 = (f32[10,1,256]{2,1,0:T(1,128)S(1)}, f32[10,1,256]{2,1,0:T(1,128)S(1)}, u32[]{:S(2)}, u32[]{:S(2)}) collective-permute-start(f32[10,1,256]{2,1,0:T(1,128)S(1)} %get-tuple-element.25), channel_id=1, source_target_pairs={{0,1},{1,2},{2,3},{3,4},{4,5},{5,6},{6,7},{7,8},{8,9},{9,10},{10,1... | collective-permute-start | bytes 30728 | tf_op jit(solution)/shard_map/ppermute | solution.py:16
  37.6 3.1 %collective-permute-done.6 = f32[10,1,256]{2,1,0:T(1,128)S(1)} collective-permute-done((f32[10,1,256]{2,1,0:T(1,128)S(1)}, f32[10,1,256]{2,1,0:T(1,128)S(1)}, u32[]{:S(2)}, u32[]{:S(2)}) %collective-permute-start.6) | collective-permute-done | bytes 10272 | tf_op jit(solution)/shard_map/ppermute | solution.py:17
  41.4 3.3 %multiply_reduce_fusion.2 = (f32[]{:T(128)}, f32[]{:T(128)}, f32[8,128,256]{2,1,0:T(8,128)S(1)}) fusion(f32[8,128,256]{2,1,0:T(8,128)S(1)} %get-tuple-element.17, f32[8,128,256]{2,1,0:T(8,128)S(1)} %get-tuple-element.18, f32[10,130,258]{2,1,0:T(8,128)S(1)} %select_maximum_fusion.4, f32[8,128,256]{2,1,0:T(8,128)S(1)} %copy-done, ...), kind=kLoop, calls=%fused_computation.84 | loop fusion | flops 10485758 | bytes 12079112 | tf_op jit(solution)/shard_map/reduce_sum | solution.py:62
  45.0 3.2 %collective-permute-start.9 = (f32[1,128,256]{2,1,0:T(8,128)S(1)}, f32[1,128,256]{2,1,0:T(8,128)S(1)}, u32[]{:S(2)}, u32[]{:S(2)}) collective-permute-start(f32[1,128,256]{2,1,0:T(8,128)S(1)} %get-tuple-element.29), channel_id=1, source_target_pairs={{0,16},{16,32},{32,48},{48,64},{64,80},{80,96},{96,112},{112,128},... | collective-permute-start | bytes 393224 | tf_op jit(solution)/shard_map/ppermute | solution.py:16
  48.2 1.9 collective-permute-start.8
  50.1 4.3 %collective-permute-done.8 = f32[1,128,256]{2,1,0:T(8,128)S(1)} collective-permute-done((f32[1,128,256]{2,1,0:T(8,128)S(1)}, f32[1,128,256]{2,1,0:T(8,128)S(1)}, u32[]{:S(2)}, u32[]{:S(2)}) %collective-permute-start.8) | collective-permute-done | bytes 131104 | tf_op jit(solution)/shard_map/ppermute | solution.py:17
  55.1 4.4 %collective-permute-start.11 = (f32[10,1,256]{2,1,0:T(1,128)}, f32[10,1,256]{2,1,0:T(1,128)S(1)}, u32[]{:S(2)}, u32[]{:S(2)}) collective-permute-start(f32[10,1,256]{2,1,0:T(1,128)} %get-tuple-element.23), channel_id=1, source_target_pairs={{0,1},{1,2},{2,3},{3,4},{4,5},{5,6},{6,7},{7,8},{8,9},{9,10},{10,1... | collective-permute-start | bytes 30728 | tf_op jit(solution)/shard_map/ppermute | solution.py:16
  60.9 31.4 %all-reduce.6 = (f32[]{:T(128)}, f32[]{:T(128)}) all-reduce(f32[]{:T(128)} %get-tuple-element.5, f32[]{:T(128)} %get-tuple-element.4), channel_id=1, replica_groups=mesh['gx'=32,'gy'=16] {'gy'}, use_global_device_ids=true, to_apply=%region_1.2 | all-reduce | flops 2 | bytes 16 | tf_op jit(solution)/shard_map/psum | solution.py:68
  92.3 58.1 %all-reduce.4 = (f32[]{:T(128)}, f32[]{:T(128)}) all-reduce(f32[]{:T(128)} %get-tuple-element.12, f32[]{:T(128)} %get-tuple-element.13), channel_id=1, replica_groups=mesh['gx'=32,'gy'=16] {'gx'}, use_global_device_ids=true, to_apply=%region_2.3 | all-reduce | flops 2 | bytes 16 | tf_op jit(solution)/shard_map/psum | solution.py:68
  151.6 2.2 select_maximum_fusion
  153.8 5.7 %multiply_reduce_fusion = (f32[]{:T(128)}, f32[]{:T(128)}, f32[8,128,256]{2,1,0:T(8,128)}) fusion(f32[8,128,256]{2,1,0:T(8,128)S(1)} %copy-done.5, f32[8,128,256]{2,1,0:T(8,128)} %copy-done.6, f32[]{:T(128)S(6)} %div.36, f32[8,128,256]{2,1,0:T(8,128)S(1)} %get-tuple-element.18, f32[10,130,258]{2,1,0:T(8,128)S(1)} %select_maximum_fusion, ...), kind=kLoop, calls=%fused_computation.81 | loop fusion | flops 11534334 | bytes 13127692 | tf_op jit(solution)/shard_map/reduce_sum | solution.py:62
  159.5 29.2 %all-reduce.5 = (f32[]{:T(128)}, f32[]{:T(128)}) all-reduce(f32[]{:T(128)} %get-tuple-element.3, f32[]{:T(128)} %get-tuple-element.2), channel_id=1, replica_groups=mesh['gx'=32,'gy'=16] {'gy'}, use_global_device_ids=true, to_apply=%region_7.8 | all-reduce | flops 2 | bytes 16 | tf_op jit(solution)/shard_map/psum | solution.py:68
  188.7 52.8 %all-reduce.3 = (f32[]{:T(128)}, f32[]{:T(128)}) all-reduce(f32[]{:T(128)} %get-tuple-element.10, f32[]{:T(128)} %get-tuple-element.11), channel_id=1, replica_groups=mesh['gx'=32,'gy'=16] {'gx'}, use_global_device_ids=true, to_apply=%region_8.9 | all-reduce | flops 2 | bytes 16 | tf_op jit(solution)/shard_map/psum | solution.py:68
  245.7 3.6 %multiply_subtract_fusion = (f32[8,128,256]{2,1,0:T(8,128)}, f32[8,128,256]{2,1,0:T(8,128)}) fusion(f32[8,128,256]{2,1,0:T(8,128)} %get-tuple-element.14, f32[8,128,256]{2,1,0:T(8,128)} %copy-done.6, f32[]{:T(128)S(6)} %div.37, f32[]{:T(128)S(6)} %div.39, f32[8,128,256]{2,1,0:T(8,128)} %copy-done.4, f32[]{:T(128)S(6)} %div.36, ...), kind=kLoop, calls=%fused_computation.79 | loop fusion | flops 3145728 | bytes 6291468 | tf_op jit(solution)/shard_map/sub | solution.py:98
  (45 shorter events, 6.0 us)
Async XLA Ops:
  1.6 10.1 %collective-permute-start.1 = (f32[1,128,256]{2,1,0:T(8,128)S(1)}, f32[1,128,256]{2,1,0:T(8,128)S(1)}, u32[]{:S(2)}, u32[]{:S(2)}) collective-permute-start(f32[1,128,256]{2,1,0:T(8,128)S(1)} %get-tuple-element.34), channel_id=1, source_target_pairs={{0,16},{16,32},{32,48},{48,64},{64,80},{80,96},{96,112},{112,128},... | collective-permute-start | bytes 393224 | tf_op jit(solution)/shard_map/ppermute | solution.py:16
  6.6 6.5 %collective-permute-start = (f32[1,128,256]{2,1,0:T(8,128)S(1)}, f32[1,128,256]{2,1,0:T(8,128)S(1)}, u32[]{:S(2)}, u32[]{:S(2)}) collective-permute-start(f32[1,128,256]{2,1,0:T(8,128)S(1)} %get-tuple-element.33), channel_id=1, source_target_pairs={{16,0},{32,16},{48,32},{64,48},{80,64},{96,80},{112,96},{128,112},... | collective-permute-start | bytes 393224 | tf_op jit(solution)/shard_map/ppermute | solution.py:17
  13.1 8.1 %copy-start = (f32[8,128,256]{2,1,0:T(8,128)S(1)}, f32[8,128,256]{2,1,0:T(8,128)}, u32[]{:S(2)}) copy-start(f32[8,128,256]{2,1,0:T(8,128)} %param.3) | copy-start | bytes 3145732
  13.1 8.1 %copy-start.11 = (f32[8,128,256]{2,1,0:T(8,128)S(1)}, f32[8,128,256]{2,1,0:T(8,128)}, u32[]{:S(2)}) copy-start(f32[8,128,256]{2,1,0:T(8,128)} %param.2) | copy-start | bytes 3145732
  13.1 4.2 %collective-permute-start.3 = (f32[10,1,256]{2,1,0:T(1,128)S(1)}, f32[10,1,256]{2,1,0:T(1,128)S(1)}, u32[]{:S(2)}, u32[]{:S(2)}) collective-permute-start(f32[10,1,256]{2,1,0:T(1,128)S(1)} %get-tuple-element.27), channel_id=1, source_target_pairs={{0,1},{1,2},{2,3},{3,4},{4,5},{5,6},{6,7},{7,8},{8,9},{9,10},{10,1... | collective-permute-start | bytes 30728 | tf_op jit(solution)/shard_map/ppermute | solution.py:16
  16.0 4.4 %collective-permute-start.2 = (f32[10,1,256]{2,1,0:T(1,128)S(1)}, f32[10,1,256]{2,1,0:T(1,128)S(1)}, u32[]{:S(2)}, u32[]{:S(2)}) collective-permute-start(f32[10,1,256]{2,1,0:T(1,128)S(1)} %get-tuple-element.28), channel_id=1, source_target_pairs={{1,0},{2,1},{3,2},{4,3},{5,4},{6,5},{7,6},{8,7},{9,8},{10,9},{11,1... | collective-permute-start | bytes 30728 | tf_op jit(solution)/shard_map/ppermute | solution.py:17
  23.4 18.0 %copy-start.4 = (f32[8,128,256]{2,1,0:T(8,128)}, f32[8,128,256]{2,1,0:T(8,128)S(1)}, u32[]{:S(2)}) copy-start(f32[8,128,256]{2,1,0:T(8,128)S(1)} %get-tuple-element.17) | copy-start | bytes 3145732
  23.4 18.0 %copy-start.7 = (f32[8,128,256]{2,1,0:T(8,128)}, f32[8,128,256]{2,1,0:T(8,128)S(1)}, u32[]{:S(2)}) copy-start(f32[8,128,256]{2,1,0:T(8,128)S(1)} %get-tuple-element.19) | copy-start | bytes 3145732
  23.4 18.0 %copy-start.8 = (f32[8,128,256]{2,1,0:T(8,128)}, f32[8,128,256]{2,1,0:T(8,128)S(1)}, u32[]{:S(2)}) copy-start(f32[8,128,256]{2,1,0:T(8,128)S(1)} %get-tuple-element.20) | copy-start | bytes 3145732
  23.5 5.3 %collective-permute-start.5 = (f32[1,128,256]{2,1,0:T(8,128)S(1)}, f32[1,128,256]{2,1,0:T(8,128)S(1)}, u32[]{:S(2)}, u32[]{:S(2)}) collective-permute-start(f32[1,128,256]{2,1,0:T(8,128)S(1)} %get-tuple-element.31), channel_id=1, source_target_pairs={{0,16},{16,32},{32,48},{48,64},{64,80},{80,96},{96,112},{112,128},... | collective-permute-start | bytes 393224 | tf_op jit(solution)/shard_map/ppermute | solution.py:16
  26.8 6.3 %collective-permute-start.4 = (f32[1,128,256]{2,1,0:T(8,128)S(1)}, f32[1,128,256]{2,1,0:T(8,128)S(1)}, u32[]{:S(2)}, u32[]{:S(2)}) collective-permute-start(f32[1,128,256]{2,1,0:T(8,128)S(1)} %get-tuple-element.32), channel_id=1, source_target_pairs={{16,0},{32,16},{48,32},{64,48},{80,64},{96,80},{112,96},{128,112},... | collective-permute-start | bytes 393224 | tf_op jit(solution)/shard_map/ppermute | solution.py:17
  33.1 4.4 %collective-permute-start.7 = (f32[10,1,256]{2,1,0:T(1,128)S(1)}, f32[10,1,256]{2,1,0:T(1,128)S(1)}, u32[]{:S(2)}, u32[]{:S(2)}) collective-permute-start(f32[10,1,256]{2,1,0:T(1,128)S(1)} %get-tuple-element.25), channel_id=1, source_target_pairs={{0,1},{1,2},{2,3},{3,4},{4,5},{5,6},{6,7},{7,8},{8,9},{9,10},{10,1... | collective-permute-start | bytes 30728 | tf_op jit(solution)/shard_map/ppermute | solution.py:16
  36.3 4.4 %collective-permute-start.6 = (f32[10,1,256]{2,1,0:T(1,128)S(1)}, f32[10,1,256]{2,1,0:T(1,128)S(1)}, u32[]{:S(2)}, u32[]{:S(2)}) collective-permute-start(f32[10,1,256]{2,1,0:T(1,128)S(1)} %get-tuple-element.26), channel_id=1, source_target_pairs={{1,0},{2,1},{3,2},{4,3},{5,4},{6,5},{7,6},{8,7},{9,8},{10,9},{11,1... | collective-permute-start | bytes 30728 | tf_op jit(solution)/shard_map/ppermute | solution.py:17
  44.8 10.4 %copy-start.6 = (f32[8,128,256]{2,1,0:T(8,128)}, f32[8,128,256]{2,1,0:T(8,128)S(1)}, u32[]{:S(2)}) copy-start(f32[8,128,256]{2,1,0:T(8,128)S(1)} %get-tuple-element.15) | copy-start | bytes 3145732
  44.9 9.5 %copy-start.2 = (f32[8,128,256]{2,1,0:T(8,128)}, f32[8,128,256]{2,1,0:T(8,128)S(1)}, u32[]{:S(2)}) copy-start(f32[8,128,256]{2,1,0:T(8,128)S(1)} %mul.118) | copy-start | bytes 3145732
  45.0 5.2 %collective-permute-start.9 = (f32[1,128,256]{2,1,0:T(8,128)S(1)}, f32[1,128,256]{2,1,0:T(8,128)S(1)}, u32[]{:S(2)}, u32[]{:S(2)}) collective-permute-start(f32[1,128,256]{2,1,0:T(8,128)S(1)} %get-tuple-element.29), channel_id=1, source_target_pairs={{0,16},{16,32},{32,48},{48,64},{64,80},{80,96},{96,112},{112,128},... | collective-permute-start | bytes 393224 | tf_op jit(solution)/shard_map/ppermute | solution.py:16
  48.2 6.3 %collective-permute-start.8 = (f32[1,128,256]{2,1,0:T(8,128)S(1)}, f32[1,128,256]{2,1,0:T(8,128)S(1)}, u32[]{:S(2)}, u32[]{:S(2)}) collective-permute-start(f32[1,128,256]{2,1,0:T(8,128)S(1)} %get-tuple-element.30), channel_id=1, source_target_pairs={{16,0},{32,16},{48,32},{64,48},{80,64},{96,80},{112,96},{128,112},... | collective-permute-start | bytes 393224 | tf_op jit(solution)/shard_map/ppermute | solution.py:17
  54.5 0.7 copy-start.9
  55.1 96.4 %collective-permute-start.11 = (f32[10,1,256]{2,1,0:T(1,128)}, f32[10,1,256]{2,1,0:T(1,128)S(1)}, u32[]{:S(2)}, u32[]{:S(2)}) collective-permute-start(f32[10,1,256]{2,1,0:T(1,128)} %get-tuple-element.23), channel_id=1, source_target_pairs={{0,1},{1,2},{2,3},{3,4},{4,5},{5,6},{6,7},{7,8},{8,9},{9,10},{10,1... | collective-permute-start | bytes 30728 | tf_op jit(solution)/shard_map/ppermute | solution.py:16
  59.6 92.0 %collective-permute-start.10 = (f32[10,1,256]{2,1,0:T(1,128)}, f32[10,1,256]{2,1,0:T(1,128)S(1)}, u32[]{:S(2)}, u32[]{:S(2)}) collective-permute-start(f32[10,1,256]{2,1,0:T(1,128)} %get-tuple-element.24), channel_id=1, source_target_pairs={{1,0},{2,1},{3,2},{4,3},{5,4},{6,5},{7,6},{8,7},{9,8},{10,9},{11,1... | collective-permute-start | bytes 30728 | tf_op jit(solution)/shard_map/ppermute | solution.py:17
  151.5 2.2 copy-start.1
  151.6 2.2 copy-start.3
  151.6 2.2 copy-start.5
  151.6 2.2 copy-start.10
